TPU v7x, 32 devices: a whole 2x2x4 slice. The times are simulated.
32 devices in a mesh: gx: 4 (over x, core), gy: 8 (over z, y).
Axes of the slice: x: 2, y: 2, z: 4, core: 2. Of those that a mesh axis runs over, the one named last changes fastest.
Arguments:
- positions: float32 [3, 4, 8, 128], P(None, 'gx', 'gy'), may hold values from 0 to 20
- spring: float32 [4, 8, 128], P('gx', 'gy'), may hold values from 0.25 to 4
- border: int32 [4, 8, 32], P('gx', 'gy'), may hold values from 0 to 127, as said below
- neighbours: int32 [4, 8, 64, 128], P('gx', 'gy'), may hold values from -1 to 1055, as said below
- vec_prev: float32 [3, 8, 4, 8, 128], P(None, None, 'gx', 'gy'), may hold values from -6 to 6
- vec_now: float32 [3, 8, 4, 8, 128], P(None, None, 'gx', 'gy'), may hold values from -6 to 6
- heat_prev: float32 [3, 8, 4, 8, 128], P(None, None, 'gx', 'gy'), may hold values from -6 to 6
- heat_now: float32 [3, 8, 4, 8, 128], P(None, None, 'gx', 'gy'), may hold values from -6 to 6
Outputs:
- vec_next: float32 [3, 8, 4, 8, 128], P(None, None, 'gx', 'gy')
- vec_after: float32 [3, 8, 4, 8, 128], P(None, None, 'gx', 'gy')
- heat_next: float32 [3, 8, 4, 8, 128], P(None, None, 'gx', 'gy')
- heat_after: float32 [3, 8, 4, 8, 128], P(None, None, 'gx', 'gy')
Inputs may be any that keep to these rules, and one draw needn't show every extreme that they name: `border`: each column's row lists 32 different atoms of that column. `neighbours`: -1 marks an empty slot, and empty slots follow the used ones; an entry o * 128 + k names for o = 4 the column's own atom k, else entry k (k < 32) of the border table of the column o // 3 - 1 steps along x and o % 3 - 1 steps along y (periodic); every atom uses at least 32 slots and some atom of every column uses all 64.
All inputs are finite; a program needn't handle non-finite values.
Results may differ from a plain program's by a relative error of at most 0.0003.
Values sent between devices are 32-bit elements; how exact they have to be, the bound alone decides.
A program may use at most 64 MiB of HBM per device.

v0:
```python
import functools

import jax
import jax.numpy as jnp
from jax import lax
from jax.experimental import pallas as pl
from jax.experimental.pallas import tpu as pltpu
from jax.sharding import PartitionSpec as P

column_edge = 20.0
reach_sq = 64.0
MESH = pl.DeviceIdType.MESH
offsets = (0, 1, 2, 3, 5, 6, 7, 8)
pairs = ((0, 0), (0, 1), (1, 1), (1, 2), (2, 2), (0, 2))


def halves(values):
    high = values.astype(jnp.bfloat16)
    return high, (values - high.astype(jnp.float32)).astype(jnp.bfloat16)


def kernel(
    count_x, count_y,
    pos_hbm, spring_hbm, border_hbm, nbr_hbm, vp_hbm, vn_hbm, hp_hbm, hn_hbm,
    vec_next, vec_after, heat_next, heat_after,
    geo_buf, border_ref, nbr_ref, field_buf, out_buf, in_buf, key_buf, amount_buf, times_buf,
    column_buf, mat_hi, mat_lo, load_sem, send_sem, recv_sem,
):
    n_slots, n_atoms = nbr_ref.shape
    n_border = border_ref.shape[1]
    groups = n_atoms // n_border
    n_vec = field_buf.shape[1] // 3
    n_rows = 2 * n_vec
    gx, gy = lax.axis_index("gx"), lax.axis_index("gy")

    def device(rank):
        dx, dy = offsets[rank] // 3 - 1, offsets[rank] % 3 - 1
        return lax.rem(gx + dx + count_x, count_x), lax.rem(gy + dy + count_y, count_y)

    barrier = pltpu.get_barrier_semaphore()
    for rank in range(8):
        pl.semaphore_signal(barrier, inc=1, device_id=device(rank), device_id_type=MESH)

    geo_buf[...] = jnp.zeros_like(geo_buf)
    moves = (
        (border_hbm, border_ref),
        (vn_hbm, field_buf.at[0]),
        (hn_hbm, field_buf.at[1]),
        (pos_hbm.at[0], geo_buf.at[0:1]),
        (pos_hbm.at[1], geo_buf.at[1:2]),
        (pos_hbm.at[2], geo_buf.at[2:3]),
        (spring_hbm, geo_buf.at[3:4]),
        (nbr_hbm, nbr_ref),
        (vp_hbm, field_buf.at[2]),
        (hp_hbm, field_buf.at[3]),
    )
    loads = [
        pltpu.make_async_copy(src, dst, load_sem.at[i]) for i, (src, dst) in enumerate(moves)
    ]
    for load in loads:
        load.start()
    for load in loads[:7]:
        load.wait()

    lane_group = lax.broadcasted_iota(jnp.int32, (n_rows, n_atoms), 1) // n_border
    chosen = jnp.concatenate([border_ref[...]] * groups, axis=1)
    chosen = jnp.broadcast_to(chosen, (n_rows, n_atoms))

    def copies(turn):
        return [
            pltpu.make_async_remote_copy(
                src_ref=out_buf.at[turn, (7 - rank) % 4],
                dst_ref=in_buf.at[turn, 7 - rank],
                send_sem=send_sem.at[turn, rank],
                recv_sem=recv_sem.at[turn, 7 - rank],
                device_id=device(rank),
                device_id_type=MESH,
            )
            for rank in range(8)
        ]

    def pack(turn, parts):
        taken = [jnp.take_along_axis(part, chosen, axis=1) for part in parts]
        for k in range(4):
            mixed = taken[0]
            for s in range(1, len(taken)):
                mixed = jnp.where(lane_group == (s + k) % 4, taken[s], mixed)
            out_buf[turn, k] = mixed

    def unpack(turn, s):
        tiles = []
        for half in range(2):
            mixed = in_buf[turn, 4 * half + (0 - s) % 4]
            for g in range(1, 4):
                mixed = jnp.where(lane_group == g, in_buf[turn, 4 * half + (g - s) % 4], mixed)
            tiles.append(pltpu.roll(mixed, (n_atoms - n_border * s) % n_atoms, 1) if s else mixed)
        return jnp.concatenate(tiles, axis=1)

    def fields(vec, heat):
        return [
            jnp.concatenate(
                [vec[a * n_vec : (a + 1) * n_vec], heat[a * n_vec : (a + 1) * n_vec]], axis=0
            )
            for a in range(3)
        ]

    geometry = geo_buf[...]
    row_of = lax.broadcasted_iota(jnp.int32, geometry.shape, 0)
    geometry = jnp.where(row_of == 3, jnp.sqrt(geometry), geometry)
    own_pos = geometry[0:3]
    root = geometry[3:4]
    state_one = fields(field_buf[0], field_buf[1])
    pack(0, state_one + [geometry])

    loads[7].wait()
    entries = nbr_ref[...]
    shift = n_atoms.bit_length() - 1
    small = n_border.bit_length() - 1
    offset = entries >> shift
    within = entries & (n_atoms - 1)
    block = jnp.where(
        offset == 4, within >> small, jnp.where(offset > 4, offset + groups - 1, offset + groups)
    )
    word = (block >> 2) * n_border + (within & (n_border - 1))
    key_buf[...] = jnp.where(entries < 0, -1, word)
    amount_buf[...] = jnp.left_shift(jnp.int32(1), (block & 3) * 8)
    n_words = 3 * n_border
    numbers = lax.broadcasted_iota(jnp.int32, (n_words, n_atoms), 0)

    def add_slots(turn, total):
        start = pl.multiple_of(turn * 8, 8)
        keys = key_buf[pl.ds(start, 8), :]
        amounts = amount_buf[pl.ds(start, 8), :]
        for n in range(8):
            total = total + jnp.where(numbers == keys[n : n + 1], amounts[n : n + 1], 0)
        return total

    words = lax.fori_loop(
        0, n_slots // 8, add_slots, jnp.zeros((n_words, n_atoms), jnp.int32)
    )
    for g in range(3):
        for f in range(4):
            row = (4 * g + f) * n_border
            part = words[g * n_border : (g + 1) * n_border]
            times_buf[row : row + n_border] = ((part >> (8 * f)) & 255).astype(jnp.float32)

    pl.semaphore_wait(barrier, 8)
    first = copies(0)
    for copy in first:
        copy.start()

    def build(turn, sums):
        group = pl.ds(pl.multiple_of(turn * n_border, n_border), n_border)
        columns = column_buf[group, :]
        delta = [columns[:, a : a + 1] - own_pos[a : a + 1] for a in range(3)]
        dist_sq = delta[0] * delta[0] + delta[1] * delta[1] + delta[2] * delta[2]
        scale = times_buf[group, :] * (columns[:, 3:4] * root)
        near = dist_sq + 1.0
        share = scale / (near * (n_slots + dist_sq * (n_slots / reach_sq)))
        coupling = share * near
        bent = [(share + share) * part for part in delta]
        out = []
        for index, (a, b) in enumerate(pairs):
            entry = bent[a] * delta[b]
            if a == b:
                entry = entry + coupling
            high, low = halves(entry)
            lanes = slice(index * n_atoms, (index + 1) * n_atoms)
            mat_hi[group, lanes] = high
            mat_lo[group, lanes] = low
            out.append(sums[index] + jnp.sum(entry.reshape(-1, 8, n_atoms), axis=0))
        return tuple(out)

    def product(rows, sources):
        high, low = halves(jnp.concatenate(sources, axis=0))
        both = jnp.concatenate([high, low], axis=0)
        big = jnp.dot(both, mat_hi[rows, :], preferred_element_type=jnp.float32)
        rest = jnp.dot(high, mat_lo[rows, :], preferred_element_type=jnp.float32)
        return big[: 3 * n_rows] + big[3 * n_rows :] + rest

    def pieces(full):
        return [
            [
                full[b * n_rows : (b + 1) * n_rows, index * n_atoms : (index + 1) * n_atoms]
                for index in range(6)
            ]
            for b in range(3)
        ]

    def gathered(full):
        part = pieces(full)
        place = {pair: index for index, pair in enumerate(pairs)}
        return [
            sum(part[b][place[(min(a, b), max(a, b))]] for b in range(3)) for a in range(3)
        ]

    sums = tuple(jnp.zeros((8, n_atoms), jnp.float32) for _ in pairs)
    column_buf[:n_atoms] = jnp.transpose(geometry[:8])
    sums = lax.fori_loop(0, groups, build, sums)
    home = slice(0, n_atoms)
    away = slice(n_atoms, 3 * n_atoms)
    near_part = product(home, state_one)

    for copy in first:
        copy.wait_recv()
    far_geometry = unpack(0, 3)[:8]
    rank_of_lane = lax.broadcasted_iota(jnp.int32, (1, 2 * n_atoms), 1) // n_border
    offset_of_lane = jnp.where(rank_of_lane >= 4, rank_of_lane + 1, rank_of_lane)
    step_x = offset_of_lane // 3 - 1
    step_y = offset_of_lane - 3 * (step_x + 1) - 1
    far_geometry = jnp.concatenate(
        [
            far_geometry[0:1] + step_x.astype(jnp.float32) * column_edge,
            far_geometry[1:2] + step_y.astype(jnp.float32) * column_edge,
            far_geometry[2:8],
        ],
        axis=0,
    )
    column_buf[n_atoms:] = jnp.transpose(far_geometry)
    sums = lax.fori_loop(groups, groups + 8, build, sums)
    totals = [jnp.sum(part, axis=0, keepdims=True) for part in sums]
    weight = {pair: total for pair, total in zip(pairs, totals)}

    def stepped(state, before, far):
        out = []
        for a in range(3):
            value = sum(weight[(min(a, b), max(a, b))] * state[b] for b in range(3))
            out.append(2.0 * (value - far[a] - state[a]) - before[a])
        return out

    far = gathered(near_part + product(away, [unpack(0, s) for s in range(3)]))
    for load in loads[8:]:
        load.wait()
    state_two = stepped(state_one, fields(field_buf[2], field_buf[3]), far)
    pack(1, state_two)
    second = copies(1)
    for copy in second:
        copy.start()
    for a in range(3):
        vec_next[a * n_vec : (a + 1) * n_vec] = state_two[a][:n_vec]
        heat_next[a * n_vec : (a + 1) * n_vec] = state_two[a][n_vec:]
    near_part = product(home, state_two)
    for copy in second:
        copy.wait_recv()
    far = gathered(near_part + product(away, [unpack(1, s) for s in range(3)]))
    state_three = stepped(state_two, state_one, far)
    for a in range(3):
        vec_after[a * n_vec : (a + 1) * n_vec] = state_three[a][:n_vec]
        heat_after[a * n_vec : (a + 1) * n_vec] = state_three[a][n_vec:]
    for copy in first + second:
        copy.wait_send()


def deliver(*refs):
    sem = refs[8]
    moves = [pltpu.make_async_copy(refs[i], refs[4 + i], sem.at[i]) for i in range(4)]
    for move in moves:
        move.start()
    for move in moves:
        move.wait()


def shards(positions, spring, border, neighbours, vec_prev, vec_now, heat_prev, heat_now):
    n_atoms = spring.shape[-1]
    n_slots = neighbours.shape[2]
    n_border = border.shape[-1]
    n_vec = vec_prev.shape[1]
    n_rows = 2 * n_vec
    flat = jax.ShapeDtypeStruct((3 * n_vec, n_atoms), jnp.float32)
    vmem = pl.BlockSpec(memory_space=pltpu.VMEM)
    hbm = pl.BlockSpec(memory_space=pltpu.HBM)
    made = pl.pallas_call(
        functools.partial(kernel, lax.axis_size("gx"), lax.axis_size("gy")),
        out_shape=(flat,) * 4,
        in_specs=[hbm] * 8,
        out_specs=(vmem,) * 4,
        scratch_shapes=[
            pltpu.VMEM((n_rows, n_atoms), jnp.float32),
            pltpu.VMEM((1, n_border), jnp.int32),
            pltpu.VMEM((n_slots, n_atoms), jnp.int32),
            pltpu.VMEM((4, 3 * n_vec, n_atoms), jnp.float32),
            pltpu.VMEM((2, 4, n_rows, n_atoms), jnp.float32),
            pltpu.VMEM((2, 8, n_rows, n_atoms), jnp.float32),
            pltpu.VMEM((n_slots, n_atoms), jnp.int32),
            pltpu.VMEM((n_slots, n_atoms), jnp.int32),
            pltpu.VMEM((3 * n_atoms, n_atoms), jnp.float32),
            pltpu.VMEM((3 * n_atoms, 8), jnp.float32),
            pltpu.VMEM((3 * n_atoms, 6 * n_atoms), jnp.bfloat16),
            pltpu.VMEM((3 * n_atoms, 6 * n_atoms), jnp.bfloat16),
            pltpu.SemaphoreType.DMA((10,)),
            pltpu.SemaphoreType.DMA((2, 8)),
            pltpu.SemaphoreType.DMA((2, 8)),
        ],
        compiler_params=pltpu.CompilerParams(
            collective_id=0, has_side_effects=True, vmem_limit_bytes=24 * 1024 * 1024
        ),
        name="chebyshev",
    )(
        *(
            pltpu.with_memory_space_constraint(x, pltpu.HBM)
            for x in (
                positions.reshape(3, 1, n_atoms),
                spring.reshape(1, n_atoms),
                border.reshape(1, n_border),
                neighbours.reshape(n_slots, n_atoms),
                *(x.reshape(3 * n_vec, n_atoms) for x in (vec_prev, vec_now, heat_prev, heat_now)),
            )
        ),
    )
    outs = pl.pallas_call(
        deliver,
        out_shape=(flat,) * 4,
        in_specs=[vmem] * 4,
        out_specs=(hbm,) * 4,
        scratch_shapes=[pltpu.SemaphoreType.DMA((4,))],
        name="deliver",
    )(*made)
    return tuple(out.reshape(vec_prev.shape) for out in outs)


def solution(mesh):
    fields = P(None, None, "gx", "gy", None)
    return jax.shard_map(
        shards,
        mesh=mesh,
        in_specs=(
            P(None, "gx", "gy", None),
            P("gx", "gy", None),
            P("gx", "gy", None),
            P("gx", "gy", None, None),
            fields,
            fields,
            fields,
            fields,
        ),
        out_specs=(fields,) * 4,
        check_vma=False,
    )
```

profile of v0, /device:TPU:1, one launch (start us, length us, event | category | flops | bytes accessed | tf_op | source)
XLA Modules:
  0.0 21.8 jit_solution(15864039930099470726)
XLA Ops:
  0.6 17.4 %chebyshev.1 = (f32[24,128]{1,0:T(8,128)S(1)}, f32[24,128]{1,0:T(8,128)S(1)}, f32[24,128]{1,0:T(8,128)S(1)}, f32[24,128]{1,0:T(8,128)S(1)}) custom-call(f32[3,1,128]{2,1,0:T(1,128)} %bitcast.25, f32[1,128]{1,0:T(1,128)} %bitcast.26, s32[1,32]{1,0:T(1,128)} %bitcast.27, s32[64,128]{1,0:T(8,128)} %bitcast.20, f32[24,128]{1,0:T(8,128)} %bitcast.21, ...), custom_call_target="tpu_custom_call" | custom-call | tf_op jit(solution)/shard_map/chebyshev/pallas_call | solution.py:272
  18.0 0.0 copy-start
  18.0 0.6 %copy-done = f32[24,128]{1,0:T(8,128)} copy-done((f32[24,128]{1,0:T(8,128)}, f32[24,128]{1,0:T(8,128)S(1)}, u32[]{:S(2)}) %copy-start) | copy-done | bytes 12312
  18.6 0.0 copy-start.1
  18.6 0.6 %copy-done.1 = f32[24,128]{1,0:T(8,128)} copy-done((f32[24,128]{1,0:T(8,128)}, f32[24,128]{1,0:T(8,128)S(1)}, u32[]{:S(2)}) %copy-start.1) | copy-done | bytes 12312
  19.2 0.0 copy-start.2
  19.2 0.6 %copy-done.2 = f32[24,128]{1,0:T(8,128)} copy-done((f32[24,128]{1,0:T(8,128)}, f32[24,128]{1,0:T(8,128)S(1)}, u32[]{:S(2)}) %copy-start.2) | copy-done | bytes 12312
  19.8 0.0 copy-start.3
  19.8 0.6 %copy-done.3 = f32[24,128]{1,0:T(8,128)} copy-done((f32[24,128]{1,0:T(8,128)}, f32[24,128]{1,0:T(8,128)S(1)}, u32[]{:S(2)}) %copy-start.3) | copy-done | bytes 12312
  20.4 1.4 %deliver.1 = (f32[24,128]{1,0:T(8,128)}, f32[24,128]{1,0:T(8,128)}, f32[24,128]{1,0:T(8,128)}, f32[24,128]{1,0:T(8,128)}) custom-call(f32[24,128]{1,0:T(8,128)} %copy-done, f32[24,128]{1,0:T(8,128)} %copy-done.1, f32[24,128]{1,0:T(8,128)} %copy-done.2, f32[24,128]{1,0:T(8,128)} %copy-done.3), custom_call_target="tpu_custom_call" | custom-call | tf_op jit(solution)/shard_map/deliver/pallas_call | solution.py:310
Async XLA Ops:
  18.0 0.6 %copy-start = (f32[24,128]{1,0:T(8,128)}, f32[24,128]{1,0:T(8,128)S(1)}, u32[]{:S(2)}) copy-start(f32[24,128]{1,0:T(8,128)S(1)} %get-tuple-element.12.refs_0_) | copy-start | bytes 36868
  18.6 0.6 %copy-start.1 = (f32[24,128]{1,0:T(8,128)}, f32[24,128]{1,0:T(8,128)S(1)}, u32[]{:S(2)}) copy-start(f32[24,128]{1,0:T(8,128)S(1)} %get-tuple-element.13.refs_1_) | copy-start | bytes 36868
  19.2 0.6 %copy-start.2 = (f32[24,128]{1,0:T(8,128)}, f32[24,128]{1,0:T(8,128)S(1)}, u32[]{:S(2)}) copy-start(f32[24,128]{1,0:T(8,128)S(1)} %get-tuple-element.14.refs_2_) | copy-start | bytes 36868
  19.8 0.6 %copy-start.3 = (f32[24,128]{1,0:T(8,128)}, f32[24,128]{1,0:T(8,128)S(1)}, u32[]{:S(2)}) copy-start(f32[24,128]{1,0:T(8,128)S(1)} %get-tuple-element.15.refs_3_) | copy-start | bytes 36868
where the time goes:
time: 22.1 us; the launch traced here: 21.8 us
  Pallas kernels  18.8 us (85%)
  local copies, waits for them, and re-layouts  2.38 us (11%)
  between operations  0.65 us (3%)
    pallas_call x1, Pallas kernels, shards(): pl.pallas_call(functools.partial(kernel, lax.axis_size('gx'), lax.axis_si...  17.4 us
    unnamed x8, local copies, waits for them, and re-layouts  2.38 us
    pallas_call x1, Pallas kernels, shards(): pl.pallas_call(deliver, out_shape=(flat,) * 4, in_specs=[vmem] * 4, out_s...  1.4 us

commit v1 on v0

--- a/solution.py
+++ b/solution.py
@@ -11,6 +11,7 @@
 reach_sq = 64.0
 MESH = pl.DeviceIdType.MESH
 offsets = (0, 1, 2, 3, 5, 6, 7, 8)
+send_order = (0, 3, 5, 2, 4, 7, 1, 6)
 pairs = ((0, 0), (0, 1), (1, 1), (1, 2), (2, 2), (0, 2))
 
 
@@ -24,7 +25,7 @@
     pos_hbm, spring_hbm, border_hbm, nbr_hbm, vp_hbm, vn_hbm, hp_hbm, hn_hbm,
     vec_next, vec_after, heat_next, heat_after,
     geo_buf, border_ref, nbr_ref, field_buf, out_buf, in_buf, key_buf, amount_buf, times_buf,
-    column_buf, mat_hi, mat_lo, load_sem, send_sem, recv_sem,
+    column_buf, turned_buf, mat_hi, mat_lo, load_sem, send_sem, recv_sem,
 ):
     n_slots, n_atoms = nbr_ref.shape
     n_border = border_ref.shape[1]
@@ -146,12 +147,17 @@
 
     pl.semaphore_wait(barrier, 8)
     first = copies(0)
-    for copy in first:
-        copy.start()
-
-    def build(turn, sums):
-        group = pl.ds(pl.multiple_of(turn * n_border, n_border), n_border)
-        columns = column_buf[group, :]
+    for rank in send_order:
+        first[rank].start()
+
+    def start_of(turn):
+        start = turn * n_border
+        return start if isinstance(turn, int) else pl.multiple_of(start, n_border)
+
+    def build(turn, sums, columns=None):
+        group = pl.ds(start_of(turn), n_border)
+        if columns is None:
+            columns = column_buf[group, :]
         delta = [columns[:, a : a + 1] - own_pos[a : a + 1] for a in range(3)]
         dist_sq = delta[0] * delta[0] + delta[1] * delta[1] + delta[2] * delta[2]
         scale = times_buf[group, :] * (columns[:, 3:4] * root)
@@ -195,29 +201,47 @@
         ]
 
     sums = tuple(jnp.zeros((8, n_atoms), jnp.float32) for _ in pairs)
-    column_buf[:n_atoms] = jnp.transpose(geometry[:8])
+    column_buf[...] = jnp.transpose(geometry[:8])
     sums = lax.fori_loop(0, groups, build, sums)
     home = slice(0, n_atoms)
     away = slice(n_atoms, 3 * n_atoms)
     near_part = product(home, state_one)
 
-    for copy in first:
-        copy.wait_recv()
-    far_geometry = unpack(0, 3)[:8]
-    rank_of_lane = lax.broadcasted_iota(jnp.int32, (1, 2 * n_atoms), 1) // n_border
-    offset_of_lane = jnp.where(rank_of_lane >= 4, rank_of_lane + 1, rank_of_lane)
-    step_x = offset_of_lane // 3 - 1
-    step_y = offset_of_lane - 3 * (step_x + 1) - 1
-    far_geometry = jnp.concatenate(
-        [
-            far_geometry[0:1] + step_x.astype(jnp.float32) * column_edge,
-            far_geometry[1:2] + step_y.astype(jnp.float32) * column_edge,
-            far_geometry[2:8],
-        ],
-        axis=0,
-    )
-    column_buf[n_atoms:] = jnp.transpose(far_geometry)
-    sums = lax.fori_loop(groups, groups + 8, build, sums)
+    lower = 2 * gy < count_y
+    order = [
+        rank if rank == other else jnp.where(lower, rank, other)
+        for rank, other in zip((1, 6, 2, 4, 7, 0, 3, 5), (1, 6, 0, 3, 5, 2, 4, 7))
+    ]
+    component = lax.broadcasted_iota(jnp.int32, (1, 8), 1)
+
+    def receive(ranks, sums):
+        for rank in ranks:
+            pltpu.make_async_remote_copy(
+                src_ref=out_buf.at[0, 0],
+                dst_ref=in_buf.at[0, rank],
+                send_sem=send_sem.at[0, 0],
+                recv_sem=recv_sem.at[0, rank],
+                device_id=device(0),
+                device_id_type=MESH,
+            ).wait_recv()
+        for place, rank in enumerate(ranks):
+            turned_buf[place] = jnp.transpose(in_buf[0, rank, :8, :])
+        for place, rank in enumerate(ranks):
+            offset = rank + (rank >= 4) if isinstance(rank, int) else rank + jnp.where(rank >= 4, 1, 0)
+            step_x = offset // 3 - 1
+            step_y = offset - 3 * (step_x + 1) - 1
+            step = jnp.where(component == 0, step_x, jnp.where(component == 1, step_y, 0))
+            group = (rank + 3) % 4
+            start = group * n_border
+            if not isinstance(rank, int):
+                start = pl.multiple_of(start, n_border)
+            columns = turned_buf[place, pl.ds(start, n_border), :]
+            columns = columns + step.astype(jnp.float32) * column_edge
+            sums = build(groups + rank, sums, columns)
+        return sums
+
+    sums = receive(order[:5], sums)
+    sums = receive(order[5:], sums)
     totals = [jnp.sum(part, axis=0, keepdims=True) for part in sums]
     weight = {pair: total for pair, total in zip(pairs, totals)}
 
@@ -234,8 +258,8 @@
     state_two = stepped(state_one, fields(field_buf[2], field_buf[3]), far)
     pack(1, state_two)
     second = copies(1)
-    for copy in second:
-        copy.start()
+    for rank in send_order:
+        second[rank].start()
     for a in range(3):
         vec_next[a * n_vec : (a + 1) * n_vec] = state_two[a][:n_vec]
         heat_next[a * n_vec : (a + 1) * n_vec] = state_two[a][n_vec:]
@@ -271,7 +295,7 @@
     hbm = pl.BlockSpec(memory_space=pltpu.HBM)
     made = pl.pallas_call(
         functools.partial(kernel, lax.axis_size("gx"), lax.axis_size("gy")),
-        out_shape=(flat,) * 4,
+        out_shape=(pltpu.VMEM(flat.shape, flat.dtype),) * 4,
         in_specs=[hbm] * 8,
         out_specs=(vmem,) * 4,
         scratch_shapes=[
@@ -284,7 +308,8 @@
             pltpu.VMEM((n_slots, n_atoms), jnp.int32),
             pltpu.VMEM((n_slots, n_atoms), jnp.int32),
             pltpu.VMEM((3 * n_atoms, n_atoms), jnp.float32),
-            pltpu.VMEM((3 * n_atoms, 8), jnp.float32),
+            pltpu.VMEM((n_atoms, 8), jnp.float32),
+            pltpu.VMEM((5, n_atoms, 8), jnp.float32),
             pltpu.VMEM((3 * n_atoms, 6 * n_atoms), jnp.bfloat16),
             pltpu.VMEM((3 * n_atoms, 6 * n_atoms), jnp.bfloat16),
             pltpu.SemaphoreType.DMA((10,)),

time: 22.1 us -> 21.2 us (0.959)
  Pallas kernels: 18.8 us -> 18 us
    pallas_call x1, Pallas kernels: 17.4 us -> 16.6 us  [shards(): pl.pallas_call(functools.partial(kernel, lax.axis_size('gx'), lax.axis_si...]
where the time goes in v1:
time: 21.2 us; the launch traced here: 21 us
  Pallas kernels  18 us (85%)
  local copies, waits for them, and re-layouts  2.38 us (11%)
  between operations  0.65 us (3%)
    pallas_call x1, Pallas kernels, shards(): pl.pallas_call(functools.partial(kernel, lax.axis_size('gx'), lax.axis_si...  16.6 us
    unnamed x8, local copies, waits for them, and re-layouts  2.38 us
    pallas_call x1, Pallas kernels, shards(): pl.pallas_call(deliver, out_shape=(flat,) * 4, in_specs=[vmem] * 4, out_s...  1.4 us

profile of v1, /device:TPU:1, one launch (start us, length us, event | category | flops | bytes accessed | tf_op | source)
XLA Modules:
  0.0 21.0 jit_solution(5761845978456983983)
XLA Ops:
  0.6 16.6 %chebyshev.1 = (f32[24,128]{1,0:T(8,128)S(1)}, f32[24,128]{1,0:T(8,128)S(1)}, f32[24,128]{1,0:T(8,128)S(1)}, f32[24,128]{1,0:T(8,128)S(1)}) custom-call(f32[3,1,128]{2,1,0:T(1,128)} %bitcast.25, f32[1,128]{1,0:T(1,128)} %bitcast.26, s32[1,32]{1,0:T(1,128)} %bitcast.27, s32[64,128]{1,0:T(8,128)} %bitcast.20, f32[24,128]{1,0:T(8,128)} %bitcast.21, ...), custom_call_target="tpu_custom_call" | custom-call | tf_op jit(solution)/shard_map/chebyshev/pallas_call | solution.py:296
  17.2 0.0 copy-start
  17.2 0.6 %copy-done = f32[24,128]{1,0:T(8,128)} copy-done((f32[24,128]{1,0:T(8,128)}, f32[24,128]{1,0:T(8,128)S(1)}, u32[]{:S(2)}) %copy-start) | copy-done | bytes 12312
  17.8 0.0 copy-start.1
  17.8 0.6 %copy-done.1 = f32[24,128]{1,0:T(8,128)} copy-done((f32[24,128]{1,0:T(8,128)}, f32[24,128]{1,0:T(8,128)S(1)}, u32[]{:S(2)}) %copy-start.1) | copy-done | bytes 12312
  18.4 0.0 copy-start.2
  18.4 0.6 %copy-done.2 = f32[24,128]{1,0:T(8,128)} copy-done((f32[24,128]{1,0:T(8,128)}, f32[24,128]{1,0:T(8,128)S(1)}, u32[]{:S(2)}) %copy-start.2) | copy-done | bytes 12312
  19.0 0.0 copy-start.3
  19.0 0.6 %copy-done.3 = f32[24,128]{1,0:T(8,128)} copy-done((f32[24,128]{1,0:T(8,128)}, f32[24,128]{1,0:T(8,128)S(1)}, u32[]{:S(2)}) %copy-start.3) | copy-done | bytes 12312
  19.6 1.4 %deliver.1 = (f32[24,128]{1,0:T(8,128)}, f32[24,128]{1,0:T(8,128)}, f32[24,128]{1,0:T(8,128)}, f32[24,128]{1,0:T(8,128)}) custom-call(f32[24,128]{1,0:T(8,128)} %copy-done, f32[24,128]{1,0:T(8,128)} %copy-done.1, f32[24,128]{1,0:T(8,128)} %copy-done.2, f32[24,128]{1,0:T(8,128)} %copy-done.3), custom_call_target="tpu_custom_call" | custom-call | tf_op jit(solution)/shard_map/deliver/pallas_call | solution.py:335
Async XLA Ops:
  17.2 0.6 %copy-start = (f32[24,128]{1,0:T(8,128)}, f32[24,128]{1,0:T(8,128)S(1)}, u32[]{:S(2)}) copy-start(f32[24,128]{1,0:T(8,128)S(1)} %get-tuple-element.12.refs_0_) | copy-start | bytes 36868
  17.8 0.6 %copy-start.1 = (f32[24,128]{1,0:T(8,128)}, f32[24,128]{1,0:T(8,128)S(1)}, u32[]{:S(2)}) copy-start(f32[24,128]{1,0:T(8,128)S(1)} %get-tuple-element.13.refs_1_) | copy-start | bytes 36868
  18.4 0.6 %copy-start.2 = (f32[24,128]{1,0:T(8,128)}, f32[24,128]{1,0:T(8,128)S(1)}, u32[]{:S(2)}) copy-start(f32[24,128]{1,0:T(8,128)S(1)} %get-tuple-element.14.refs_2_) | copy-start | bytes 36868
  19.0 0.6 %copy-start.3 = (f32[24,128]{1,0:T(8,128)}, f32[24,128]{1,0:T(8,128)S(1)}, u32[]{:S(2)}) copy-start(f32[24,128]{1,0:T(8,128)S(1)} %get-tuple-element.15.refs_3_) | copy-start | bytes 36868

commit v2 on v1

--- a/solution.py
+++ b/solution.py
@@ -39,7 +39,7 @@
         return lax.rem(gx + dx + count_x, count_x), lax.rem(gy + dy + count_y, count_y)
 
     barrier = pltpu.get_barrier_semaphore()
-    for rank in range(8):
+    for rank in send_order:
         pl.semaphore_signal(barrier, inc=1, device_id=device(rank), device_id_type=MESH)
 
     geo_buf[...] = jnp.zeros_like(geo_buf)
@@ -339,7 +339,7 @@
         out_specs=(hbm,) * 4,
         scratch_shapes=[pltpu.SemaphoreType.DMA((4,))],
         name="deliver",
-    )(*made)
+    )(*(pltpu.with_memory_space_constraint(x, pltpu.VMEM) for x in made))
     return tuple(out.reshape(vec_prev.shape) for out in outs)
 
 

time: 21.2 us -> 18.1 us (0.85)
  local copies, waits for them, and re-layouts: 2.38 us -> 0 us
  Pallas kernels: 18 us -> 17.2 us
    unnamed x8 -> x0, local copies, waits for them, and re-layouts: 2.38 us -> none
    pallas_call x1, Pallas kernels: 1.4 us -> 0.65 us  [shards(): pl.pallas_call(deliver, out_shape=(flat,) * 4, in_specs=[vmem] * 4, out_s...]
where the time goes in v2:
time: 18.1 us; the launch traced here: 17.9 us
  Pallas kernels  17.2 us (95%)
  between operations  0.64 us (4%)
    pallas_call x1, Pallas kernels, shards(): pl.pallas_call(functools.partial(kernel, lax.axis_size('gx'), lax.axis_si...  16.6 us
    pallas_call x1, Pallas kernels, shards(): pl.pallas_call(deliver, out_shape=(flat,) * 4, in_specs=[vmem] * 4, out_s...  0.65 us

profile of v2, /device:TPU:1, one launch (start us, length us, event | category | flops | bytes accessed | tf_op | source)
XLA Modules:
  0.0 17.9 jit_solution(11576770676963590321)
XLA Ops:
  0.6 16.6 %chebyshev.1 = (f32[24,128]{1,0:T(8,128)S(1)}, f32[24,128]{1,0:T(8,128)S(1)}, f32[24,128]{1,0:T(8,128)S(1)}, f32[24,128]{1,0:T(8,128)S(1)}) custom-call(f32[3,1,128]{2,1,0:T(1,128)} %bitcast.25, f32[1,128]{1,0:T(1,128)} %bitcast.26, s32[1,32]{1,0:T(1,128)} %bitcast.27, s32[64,128]{1,0:T(8,128)} %bitcast.20, f32[24,128]{1,0:T(8,128)} %bitcast.21, ...), custom_call_target="tpu_custom_call" | custom-call | tf_op jit(solution)/shard_map/chebyshev/pallas_call | solution.py:296
  17.2 0.7 %deliver.1 = (f32[24,128]{1,0:T(8,128)}, f32[24,128]{1,0:T(8,128)}, f32[24,128]{1,0:T(8,128)}, f32[24,128]{1,0:T(8,128)}) custom-call(f32[24,128]{1,0:T(8,128)S(1)} %get-tuple-element.12.refs_0_, f32[24,128]{1,0:T(8,128)S(1)} %get-tuple-element.13.refs_1_, f32[24,128]{1,0:T(8,128)S(1)} %get-tuple-element.14.refs_2_, f32[24,128]{1,0:T(8,128)S(1)} %get-tuple-element.15.refs_3_), custom_call_target="tpu_custom_call" | custom-call | tf_op jit(solution)/shard_map/deliver/pallas_call | solution.py:335

commit v3 on v2

--- a/solution.py
+++ b/solution.py
@@ -12,6 +12,7 @@
 MESH = pl.DeviceIdType.MESH
 offsets = (0, 1, 2, 3, 5, 6, 7, 8)
 send_order = (0, 3, 5, 2, 4, 7, 1, 6)
+arrivals = ((1, 6, 2, 4, 7, 0, 3, 5), (1, 6, 0, 3, 5, 2, 4, 7))
 pairs = ((0, 0), (0, 1), (1, 1), (1, 2), (2, 2), (0, 2))
 
 
@@ -25,7 +26,7 @@
     pos_hbm, spring_hbm, border_hbm, nbr_hbm, vp_hbm, vn_hbm, hp_hbm, hn_hbm,
     vec_next, vec_after, heat_next, heat_after,
     geo_buf, border_ref, nbr_ref, field_buf, out_buf, in_buf, key_buf, amount_buf, times_buf,
-    column_buf, turned_buf, mat_hi, mat_lo, load_sem, send_sem, recv_sem,
+    column_buf, mat_hi, mat_lo, load_sem, send_sem, recv_sem,
 ):
     n_slots, n_atoms = nbr_ref.shape
     n_border = border_ref.shape[1]
@@ -70,15 +71,34 @@
     def copies(turn):
         return [
             pltpu.make_async_remote_copy(
-                src_ref=out_buf.at[turn, (7 - rank) % 4],
-                dst_ref=in_buf.at[turn, 7 - rank],
+                src_ref=out_buf.at[turn, place % 4],
+                dst_ref=in_buf.at[turn, place],
                 send_sem=send_sem.at[turn, rank],
-                recv_sem=recv_sem.at[turn, 7 - rank],
+                recv_sem=recv_sem.at[turn, place],
                 device_id=device(rank),
                 device_id_type=MESH,
             )
-            for rank in range(8)
+            for rank, place in enumerate(places)
         ]
+
+    def either(low, one, other):
+        return one if one == other else jnp.where(low, one, other)
+
+    places = [
+        either(2 * device(rank)[1] < count_y, *(order.index(7 - rank) for order in arrivals))
+        for rank in range(8)
+    ]
+
+    def arrive(turn, first, last):
+        for place in range(first, last):
+            pltpu.make_async_remote_copy(
+                src_ref=out_buf.at[turn, 0],
+                dst_ref=in_buf.at[turn, place],
+                send_sem=send_sem.at[turn, 0],
+                recv_sem=recv_sem.at[turn, place],
+                device_id=device(0),
+                device_id_type=MESH,
+            ).wait_recv()
 
     def pack(turn, parts):
         taken = [jnp.take_along_axis(part, chosen, axis=1) for part in parts]
@@ -88,14 +108,14 @@
                 mixed = jnp.where(lane_group == (s + k) % 4, taken[s], mixed)
             out_buf[turn, k] = mixed
 
-    def unpack(turn, s):
+    def unpack(turn, half):
         tiles = []
-        for half in range(2):
+        for s in range(3):
             mixed = in_buf[turn, 4 * half + (0 - s) % 4]
             for g in range(1, 4):
                 mixed = jnp.where(lane_group == g, in_buf[turn, 4 * half + (g - s) % 4], mixed)
             tiles.append(pltpu.roll(mixed, (n_atoms - n_border * s) % n_atoms, 1) if s else mixed)
-        return jnp.concatenate(tiles, axis=1)
+        return tiles
 
     def fields(vec, heat):
         return [
@@ -150,17 +170,14 @@
     for rank in send_order:
         first[rank].start()
 
-    def start_of(turn):
+    def slots_of(turn):
         start = turn * n_border
-        return start if isinstance(turn, int) else pl.multiple_of(start, n_border)
-
-    def build(turn, sums, columns=None):
-        group = pl.ds(start_of(turn), n_border)
-        if columns is None:
-            columns = column_buf[group, :]
+        return pl.ds(start if isinstance(turn, int) else pl.multiple_of(start, n_border), n_border)
+
+    def build(group, counts, columns, sums):
         delta = [columns[:, a : a + 1] - own_pos[a : a + 1] for a in range(3)]
         dist_sq = delta[0] * delta[0] + delta[1] * delta[1] + delta[2] * delta[2]
-        scale = times_buf[group, :] * (columns[:, 3:4] * root)
+        scale = times_buf[counts, :] * (columns[:, 3:4] * root)
         near = dist_sq + 1.0
         share = scale / (near * (n_slots + dist_sq * (n_slots / reach_sq)))
         coupling = share * near
@@ -177,7 +194,8 @@
             out.append(sums[index] + jnp.sum(entry.reshape(-1, 8, n_atoms), axis=0))
         return tuple(out)
 
-    def product(rows, sources):
+    def product(tile, sources):
+        rows = slice(tile * n_atoms, (tile + 1) * n_atoms)
         high, low = halves(jnp.concatenate(sources, axis=0))
         both = jnp.concatenate([high, low], axis=0)
         big = jnp.dot(both, mat_hi[rows, :], preferred_element_type=jnp.float32)
@@ -202,46 +220,35 @@
 
     sums = tuple(jnp.zeros((8, n_atoms), jnp.float32) for _ in pairs)
     column_buf[...] = jnp.transpose(geometry[:8])
-    sums = lax.fori_loop(0, groups, build, sums)
-    home = slice(0, n_atoms)
-    away = slice(n_atoms, 3 * n_atoms)
-    near_part = product(home, state_one)
+
+    def build_own(turn, sums):
+        group = slots_of(turn)
+        return build(group, group, column_buf[group, :], sums)
+
+    sums = lax.fori_loop(0, groups, build_own, sums)
+    total = product(0, state_one)
 
     lower = 2 * gy < count_y
-    order = [
-        rank if rank == other else jnp.where(lower, rank, other)
-        for rank, other in zip((1, 6, 2, 4, 7, 0, 3, 5), (1, 6, 0, 3, 5, 2, 4, 7))
-    ]
     component = lax.broadcasted_iota(jnp.int32, (1, 8), 1)
 
-    def receive(ranks, sums):
-        for rank in ranks:
-            pltpu.make_async_remote_copy(
-                src_ref=out_buf.at[0, 0],
-                dst_ref=in_buf.at[0, rank],
-                send_sem=send_sem.at[0, 0],
-                recv_sem=recv_sem.at[0, rank],
-                device_id=device(0),
-                device_id_type=MESH,
-            ).wait_recv()
-        for place, rank in enumerate(ranks):
-            turned_buf[place] = jnp.transpose(in_buf[0, rank, :8, :])
-        for place, rank in enumerate(ranks):
-            offset = rank + (rank >= 4) if isinstance(rank, int) else rank + jnp.where(rank >= 4, 1, 0)
+    def receive(first, last, sums):
+        arrive(0, first, last)
+        turned = [jnp.transpose(in_buf[0, place, :8, :]) for place in range(first, last)]
+        for place in range(first, last):
+            rank = either(lower, *(order[place] for order in arrivals))
+            offset = rank + jnp.where(jnp.int32(rank) >= 4, 1, 0)
             step_x = offset // 3 - 1
             step_y = offset - 3 * (step_x + 1) - 1
             step = jnp.where(component == 0, step_x, jnp.where(component == 1, step_y, 0))
-            group = (rank + 3) % 4
-            start = group * n_border
-            if not isinstance(rank, int):
-                start = pl.multiple_of(start, n_border)
-            columns = turned_buf[place, pl.ds(start, n_border), :]
+            start = (place + 3) % 4 * n_border
+            columns = turned[place - first][start : start + n_border]
             columns = columns + step.astype(jnp.float32) * column_edge
-            sums = build(groups + rank, sums, columns)
+            sums = build(slots_of(groups + place), slots_of(groups + rank), columns, sums)
         return sums
 
-    sums = receive(order[:5], sums)
-    sums = receive(order[5:], sums)
+    sums = receive(0, 5, sums)
+    total = total + product(1, unpack(0, 0))
+    sums = receive(5, 8, sums)
     totals = [jnp.sum(part, axis=0, keepdims=True) for part in sums]
     weight = {pair: total for pair, total in zip(pairs, totals)}
 
@@ -252,7 +259,7 @@
             out.append(2.0 * (value - far[a] - state[a]) - before[a])
         return out
 
-    far = gathered(near_part + product(away, [unpack(0, s) for s in range(3)]))
+    far = gathered(total + product(2, unpack(0, 1)))
     for load in loads[8:]:
         load.wait()
     state_two = stepped(state_one, fields(field_buf[2], field_buf[3]), far)
@@ -263,10 +270,11 @@
     for a in range(3):
         vec_next[a * n_vec : (a + 1) * n_vec] = state_two[a][:n_vec]
         heat_next[a * n_vec : (a + 1) * n_vec] = state_two[a][n_vec:]
-    near_part = product(home, state_two)
-    for copy in second:
-        copy.wait_recv()
-    far = gathered(near_part + product(away, [unpack(1, s) for s in range(3)]))
+    total = product(0, state_two)
+    arrive(1, 0, 4)
+    total = total + product(1, unpack(1, 0))
+    arrive(1, 4, 8)
+    far = gathered(total + product(2, unpack(1, 1)))
     state_three = stepped(state_two, state_one, far)
     for a in range(3):
         vec_after[a * n_vec : (a + 1) * n_vec] = state_three[a][:n_vec]
@@ -309,7 +317,6 @@
             pltpu.VMEM((n_slots, n_atoms), jnp.int32),
             pltpu.VMEM((3 * n_atoms, n_atoms), jnp.float32),
             pltpu.VMEM((n_atoms, 8), jnp.float32),
-            pltpu.VMEM((5, n_atoms, 8), jnp.float32),
             pltpu.VMEM((3 * n_atoms, 6 * n_atoms), jnp.bfloat16),
             pltpu.VMEM((3 * n_atoms, 6 * n_atoms), jnp.bfloat16),
             pltpu.SemaphoreType.DMA((10,)),

time: 18.1 us -> 17.9 us (0.989)
  Pallas kernels: 17.2 us -> 17 us
    pallas_call x1, Pallas kernels: 16.6 us -> 16.4 us  [shards(): pl.pallas_call(functools.partial(kernel, lax.axis_size('gx'), lax.axis_si...]
where the time goes in v3:
time: 17.9 us; the launch traced here: 17.7 us
  Pallas kernels  17 us (95%)
  between operations  0.64 us (4%)
    pallas_call x1, Pallas kernels, shards(): pl.pallas_call(functools.partial(kernel, lax.axis_size('gx'), lax.axis_si...  16.4 us
    pallas_call x1, Pallas kernels, shards(): pl.pallas_call(deliver, out_shape=(flat,) * 4, in_specs=[vmem] * 4, out_s...  0.65 us

profile of v3, /device:TPU:1, one launch (start us, length us, event | category | flops | bytes accessed | tf_op | source)
XLA Modules:
  0.0 17.7 jit_solution(18306186325338714403)
XLA Ops:
  0.6 16.4 %chebyshev.1 = (f32[24,128]{1,0:T(8,128)S(1)}, f32[24,128]{1,0:T(8,128)S(1)}, f32[24,128]{1,0:T(8,128)S(1)}, f32[24,128]{1,0:T(8,128)S(1)}) custom-call(f32[3,1,128]{2,1,0:T(1,128)} %bitcast.25, f32[1,128]{1,0:T(1,128)} %bitcast.26, s32[1,32]{1,0:T(1,128)} %bitcast.27, s32[64,128]{1,0:T(8,128)} %bitcast.20, f32[24,128]{1,0:T(8,128)} %bitcast.21, ...), custom_call_target="tpu_custom_call" | custom-call | tf_op jit(solution)/shard_map/chebyshev/pallas_call | solution.py:304
  17.0 0.7 %deliver.1 = (f32[24,128]{1,0:T(8,128)}, f32[24,128]{1,0:T(8,128)}, f32[24,128]{1,0:T(8,128)}, f32[24,128]{1,0:T(8,128)}) custom-call(f32[24,128]{1,0:T(8,128)S(1)} %get-tuple-element.12.refs_0_, f32[24,128]{1,0:T(8,128)S(1)} %get-tuple-element.13.refs_1_, f32[24,128]{1,0:T(8,128)S(1)} %get-tuple-element.14.refs_2_, f32[24,128]{1,0:T(8,128)S(1)} %get-tuple-element.15.refs_3_), custom_call_target="tpu_custom_call" | custom-call | tf_op jit(solution)/shard_map/deliver/pallas_call | solution.py:342

commit v4 on v3

--- a/solution.py
+++ b/solution.py
@@ -11,7 +11,7 @@
 reach_sq = 64.0
 MESH = pl.DeviceIdType.MESH
 offsets = (0, 1, 2, 3, 5, 6, 7, 8)
-send_order = (0, 3, 5, 2, 4, 7, 1, 6)
+departures = (5, 6, 7, 2, 3, 4, 0, 1)
 arrivals = ((1, 6, 2, 4, 7, 0, 3, 5), (1, 6, 0, 3, 5, 2, 4, 7))
 pairs = ((0, 0), (0, 1), (1, 1), (1, 2), (2, 2), (0, 2))
 
@@ -26,7 +26,7 @@
     pos_hbm, spring_hbm, border_hbm, nbr_hbm, vp_hbm, vn_hbm, hp_hbm, hn_hbm,
     vec_next, vec_after, heat_next, heat_after,
     geo_buf, border_ref, nbr_ref, field_buf, out_buf, in_buf, key_buf, amount_buf, times_buf,
-    column_buf, mat_hi, mat_lo, load_sem, send_sem, recv_sem,
+    mat_hi, mat_lo, load_sem, send_sem, recv_sem,
 ):
     n_slots, n_atoms = nbr_ref.shape
     n_border = border_ref.shape[1]
@@ -39,9 +39,28 @@
         dx, dy = offsets[rank] // 3 - 1, offsets[rank] % 3 - 1
         return lax.rem(gx + dx + count_x, count_x), lax.rem(gy + dy + count_y, count_y)
 
+    def either(low, one, other):
+        return one if isinstance(one, int) and one == other else jnp.where(low, one, other)
+
+    lower = 2 * gy < count_y
+    places = [
+        either(2 * device(rank)[1] < count_y, *(order.index(7 - rank) for order in arrivals))
+        for rank in range(8)
+    ]
+    targets = []
+    for turn in departures:
+        one, other = (order[turn] for order in arrivals)
+        if one == other:
+            targets.append((device(one), places[one]))
+        else:
+            targets.append((
+                tuple(jnp.where(lower, x, y) for x, y in zip(device(one), device(other))),
+                jnp.where(lower, places[one], places[other]),
+            ))
+
     barrier = pltpu.get_barrier_semaphore()
-    for rank in send_order:
-        pl.semaphore_signal(barrier, inc=1, device_id=device(rank), device_id_type=MESH)
+    for target, _ in targets:
+        pl.semaphore_signal(barrier, inc=1, device_id=target, device_id_type=MESH)
 
     geo_buf[...] = jnp.zeros_like(geo_buf)
     moves = (
@@ -73,21 +92,13 @@
             pltpu.make_async_remote_copy(
                 src_ref=out_buf.at[turn, place % 4],
                 dst_ref=in_buf.at[turn, place],
-                send_sem=send_sem.at[turn, rank],
+                send_sem=send_sem.at[turn, index],
                 recv_sem=recv_sem.at[turn, place],
-                device_id=device(rank),
+                device_id=target,
                 device_id_type=MESH,
             )
-            for rank, place in enumerate(places)
+            for index, (target, place) in enumerate(targets)
         ]
-
-    def either(low, one, other):
-        return one if one == other else jnp.where(low, one, other)
-
-    places = [
-        either(2 * device(rank)[1] < count_y, *(order.index(7 - rank) for order in arrivals))
-        for rank in range(8)
-    ]
 
     def arrive(turn, first, last):
         for place in range(first, last):
@@ -167,8 +178,8 @@
 
     pl.semaphore_wait(barrier, 8)
     first = copies(0)
-    for rank in send_order:
-        first[rank].start()
+    for copy in first:
+        copy.start()
 
     def slots_of(turn):
         start = turn * n_border
@@ -219,16 +230,12 @@
         ]
 
     sums = tuple(jnp.zeros((8, n_atoms), jnp.float32) for _ in pairs)
-    column_buf[...] = jnp.transpose(geometry[:8])
-
-    def build_own(turn, sums):
+    columns = jnp.transpose(geometry[:8])
+    for turn in range(groups):
         group = slots_of(turn)
-        return build(group, group, column_buf[group, :], sums)
-
-    sums = lax.fori_loop(0, groups, build_own, sums)
+        sums = build(group, group, columns[turn * n_border : (turn + 1) * n_border], sums)
     total = product(0, state_one)
 
-    lower = 2 * gy < count_y
     component = lax.broadcasted_iota(jnp.int32, (1, 8), 1)
 
     def receive(first, last, sums):
@@ -265,8 +272,8 @@
     state_two = stepped(state_one, fields(field_buf[2], field_buf[3]), far)
     pack(1, state_two)
     second = copies(1)
-    for rank in send_order:
-        second[rank].start()
+    for copy in second:
+        copy.start()
     for a in range(3):
         vec_next[a * n_vec : (a + 1) * n_vec] = state_two[a][:n_vec]
         heat_next[a * n_vec : (a + 1) * n_vec] = state_two[a][n_vec:]
@@ -316,7 +323,6 @@
             pltpu.VMEM((n_slots, n_atoms), jnp.int32),
             pltpu.VMEM((n_slots, n_atoms), jnp.int32),
             pltpu.VMEM((3 * n_atoms, n_atoms), jnp.float32),
-            pltpu.VMEM((n_atoms, 8), jnp.float32),
             pltpu.VMEM((3 * n_atoms, 6 * n_atoms), jnp.bfloat16),
             pltpu.VMEM((3 * n_atoms, 6 * n_atoms), jnp.bfloat16),
             pltpu.SemaphoreType.DMA((10,)),

time: 17.9 us -> 17.9 us (level)
  no operation moved by 1% of the time
where the time goes in v4:
time: 17.9 us; the launch traced here: 17.7 us
  Pallas kernels  17 us (95%)
  between operations  0.64 us (4%)
    pallas_call x1, Pallas kernels, shards(): pl.pallas_call(functools.partial(kernel, lax.axis_size('gx'), lax.axis_si...  16.4 us
    pallas_call x1, Pallas kernels, shards(): pl.pallas_call(deliver, out_shape=(flat,) * 4, in_specs=[vmem] * 4, out_s...  0.65 us

profile of v4, /device:TPU:1, one launch (start us, length us, event | category | flops | bytes accessed | tf_op | source)
XLA Modules:
  0.0 17.7 jit_solution(16175607848211407930)
XLA Ops:
  0.6 16.4 %chebyshev.1 = (f32[24,128]{1,0:T(8,128)S(1)}, f32[24,128]{1,0:T(8,128)S(1)}, f32[24,128]{1,0:T(8,128)S(1)}, f32[24,128]{1,0:T(8,128)S(1)}) custom-call(f32[3,1,128]{2,1,0:T(1,128)} %bitcast.25, f32[1,128]{1,0:T(1,128)} %bitcast.26, s32[1,32]{1,0:T(1,128)} %bitcast.27, s32[64,128]{1,0:T(8,128)} %bitcast.20, f32[24,128]{1,0:T(8,128)} %bitcast.21, ...), custom_call_target="tpu_custom_call" | custom-call | tf_op jit(solution)/shard_map/chebyshev/pallas_call | solution.py:311
  17.0 0.7 %deliver.1 = (f32[24,128]{1,0:T(8,128)}, f32[24,128]{1,0:T(8,128)}, f32[24,128]{1,0:T(8,128)}, f32[24,128]{1,0:T(8,128)}) custom-call(f32[24,128]{1,0:T(8,128)S(1)} %get-tuple-element.12.refs_0_, f32[24,128]{1,0:T(8,128)S(1)} %get-tuple-element.13.refs_1_, f32[24,128]{1,0:T(8,128)S(1)} %get-tuple-element.14.refs_2_, f32[24,128]{1,0:T(8,128)S(1)} %get-tuple-element.15.refs_3_), custom_call_target="tpu_custom_call" | custom-call | tf_op jit(solution)/shard_map/deliver/pallas_call | solution.py:348

commit v5 on v4

--- a/solution.py
+++ b/solution.py
@@ -26,7 +26,7 @@
     pos_hbm, spring_hbm, border_hbm, nbr_hbm, vp_hbm, vn_hbm, hp_hbm, hn_hbm,
     vec_next, vec_after, heat_next, heat_after,
     geo_buf, border_ref, nbr_ref, field_buf, out_buf, in_buf, key_buf, amount_buf, times_buf,
-    mat_hi, mat_lo, load_sem, send_sem, recv_sem,
+    mat_buf, load_sem, send_sem, recv_sem,
 ):
     n_slots, n_atoms = nbr_ref.shape
     n_border = border_ref.shape[1]
@@ -185,7 +185,8 @@
         start = turn * n_border
         return pl.ds(start if isinstance(turn, int) else pl.multiple_of(start, n_border), n_border)
 
-    def build(group, counts, columns, sums):
+    def build(turn, counts, columns, sums):
+        tile, row = turn // groups, turn % groups * n_border
         delta = [columns[:, a : a + 1] - own_pos[a : a + 1] for a in range(3)]
         dist_sq = delta[0] * delta[0] + delta[1] * delta[1] + delta[2] * delta[2]
         scale = times_buf[counts, :] * (columns[:, 3:4] * root)
@@ -200,18 +201,17 @@
                 entry = entry + coupling
             high, low = halves(entry)
             lanes = slice(index * n_atoms, (index + 1) * n_atoms)
-            mat_hi[group, lanes] = high
-            mat_lo[group, lanes] = low
+            mat_buf[tile, row : row + n_border, lanes] = high
+            mat_buf[tile, n_atoms + row : n_atoms + row + n_border, lanes] = low
             out.append(sums[index] + jnp.sum(entry.reshape(-1, 8, n_atoms), axis=0))
         return tuple(out)
 
     def product(tile, sources):
-        rows = slice(tile * n_atoms, (tile + 1) * n_atoms)
         high, low = halves(jnp.concatenate(sources, axis=0))
         both = jnp.concatenate([high, low], axis=0)
-        big = jnp.dot(both, mat_hi[rows, :], preferred_element_type=jnp.float32)
-        rest = jnp.dot(high, mat_lo[rows, :], preferred_element_type=jnp.float32)
-        return big[: 3 * n_rows] + big[3 * n_rows :] + rest
+        both = jnp.concatenate([both, both], axis=1)
+        full = jnp.dot(both, mat_buf[tile], preferred_element_type=jnp.float32)
+        return full[: 3 * n_rows] + full[3 * n_rows :]
 
     def pieces(full):
         return [
@@ -232,8 +232,8 @@
     sums = tuple(jnp.zeros((8, n_atoms), jnp.float32) for _ in pairs)
     columns = jnp.transpose(geometry[:8])
     for turn in range(groups):
-        group = slots_of(turn)
-        sums = build(group, group, columns[turn * n_border : (turn + 1) * n_border], sums)
+        own = columns[turn * n_border : (turn + 1) * n_border]
+        sums = build(turn, slots_of(turn), own, sums)
     total = product(0, state_one)
 
     component = lax.broadcasted_iota(jnp.int32, (1, 8), 1)
@@ -250,7 +250,7 @@
             start = (place + 3) % 4 * n_border
             columns = turned[place - first][start : start + n_border]
             columns = columns + step.astype(jnp.float32) * column_edge
-            sums = build(slots_of(groups + place), slots_of(groups + rank), columns, sums)
+            sums = build(groups + place, slots_of(groups + rank), columns, sums)
         return sums
 
     sums = receive(0, 5, sums)
@@ -323,8 +323,7 @@
             pltpu.VMEM((n_slots, n_atoms), jnp.int32),
             pltpu.VMEM((n_slots, n_atoms), jnp.int32),
             pltpu.VMEM((3 * n_atoms, n_atoms), jnp.float32),
-            pltpu.VMEM((3 * n_atoms, 6 * n_atoms), jnp.bfloat16),
-            pltpu.VMEM((3 * n_atoms, 6 * n_atoms), jnp.bfloat16),
+            pltpu.VMEM((3, 2 * n_atoms, 6 * n_atoms), jnp.bfloat16),
             pltpu.SemaphoreType.DMA((10,)),
             pltpu.SemaphoreType.DMA((2, 8)),
             pltpu.SemaphoreType.DMA((2, 8)),

time: 17.9 us -> 17.8 us (level)
  no operation moved by 1% of the time
where the time goes in v5:
time: 17.8 us; the launch traced here: 17.6 us
  Pallas kernels  17 us (96%)
  between operations  0.64 us (4%)
    pallas_call x1, Pallas kernels, shards(): pl.pallas_call(functools.partial(kernel, lax.axis_size('gx'), lax.axis_si...  16.3 us
    pallas_call x1, Pallas kernels, shards(): pl.pallas_call(deliver, out_shape=(flat,) * 4, in_specs=[vmem] * 4, out_s...  0.65 us

profile of v5, /device:TPU:1, one launch (start us, length us, event | category | flops | bytes accessed | tf_op | source)
XLA Modules:
  0.0 17.6 jit_solution(5305529709604559284)
XLA Ops:
  0.6 16.3 %chebyshev.1 = (f32[24,128]{1,0:T(8,128)S(1)}, f32[24,128]{1,0:T(8,128)S(1)}, f32[24,128]{1,0:T(8,128)S(1)}, f32[24,128]{1,0:T(8,128)S(1)}) custom-call(f32[3,1,128]{2,1,0:T(1,128)} %bitcast.25, f32[1,128]{1,0:T(1,128)} %bitcast.26, s32[1,32]{1,0:T(1,128)} %bitcast.27, s32[64,128]{1,0:T(8,128)} %bitcast.20, f32[24,128]{1,0:T(8,128)} %bitcast.21, ...), custom_call_target="tpu_custom_call" | custom-call | tf_op jit(solution)/shard_map/chebyshev/pallas_call | solution.py:311
  17.0 0.7 %deliver.1 = (f32[24,128]{1,0:T(8,128)}, f32[24,128]{1,0:T(8,128)}, f32[24,128]{1,0:T(8,128)}, f32[24,128]{1,0:T(8,128)}) custom-call(f32[24,128]{1,0:T(8,128)S(1)} %get-tuple-element.12.refs_0_, f32[24,128]{1,0:T(8,128)S(1)} %get-tuple-element.13.refs_1_, f32[24,128]{1,0:T(8,128)S(1)} %get-tuple-element.14.refs_2_, f32[24,128]{1,0:T(8,128)S(1)} %get-tuple-element.15.refs_3_), custom_call_target="tpu_custom_call" | custom-call | tf_op jit(solution)/shard_map/deliver/pallas_call | solution.py:347

commit v6 on v5

--- a/solution.py
+++ b/solution.py
@@ -181,15 +181,27 @@
     for copy in first:
         copy.start()
 
+    picked = lax.broadcasted_iota(jnp.int32, (24, 4 * n_atoms), 0) % 8
+    lane_part = lax.broadcasted_iota(jnp.int32, (24, 4 * n_atoms), 1) // n_atoms
+    selector = (picked == lane_part).astype(jnp.float32).astype(jnp.bfloat16)
+
+    def turned(rows):
+        high = rows.astype(jnp.bfloat16).astype(jnp.float32)
+        middle = (rows - high).astype(jnp.bfloat16).astype(jnp.float32)
+        parts = jnp.concatenate([high, middle, rows - high - middle], axis=0)
+        return jnp.transpose(parts).astype(jnp.bfloat16)
+
     def slots_of(turn):
         start = turn * n_border
         return pl.ds(start if isinstance(turn, int) else pl.multiple_of(start, n_border), n_border)
 
     def build(turn, counts, columns, sums):
         tile, row = turn // groups, turn % groups * n_border
-        delta = [columns[:, a : a + 1] - own_pos[a : a + 1] for a in range(3)]
+        spread = jnp.dot(columns, selector, preferred_element_type=jnp.float32)
+        wide = [spread[:, a * n_atoms : (a + 1) * n_atoms] for a in range(4)]
+        delta = [wide[a] - own_pos[a : a + 1] for a in range(3)]
         dist_sq = delta[0] * delta[0] + delta[1] * delta[1] + delta[2] * delta[2]
-        scale = times_buf[counts, :] * (columns[:, 3:4] * root)
+        scale = times_buf[counts, :] * (wide[3] * root)
         near = dist_sq + 1.0
         share = scale / (near * (n_slots + dist_sq * (n_slots / reach_sq)))
         coupling = share * near
@@ -230,17 +242,16 @@
         ]
 
     sums = tuple(jnp.zeros((8, n_atoms), jnp.float32) for _ in pairs)
-    columns = jnp.transpose(geometry[:8])
+    columns = turned(geometry[:8])
     for turn in range(groups):
         own = columns[turn * n_border : (turn + 1) * n_border]
         sums = build(turn, slots_of(turn), own, sums)
     total = product(0, state_one)
 
-    component = lax.broadcasted_iota(jnp.int32, (1, 8), 1)
+    component = lax.broadcasted_iota(jnp.int32, (8, n_atoms), 0)
 
     def receive(first, last, sums):
         arrive(0, first, last)
-        turned = [jnp.transpose(in_buf[0, place, :8, :]) for place in range(first, last)]
         for place in range(first, last):
             rank = either(lower, *(order[place] for order in arrivals))
             offset = rank + jnp.where(jnp.int32(rank) >= 4, 1, 0)
@@ -248,8 +259,8 @@
             step_y = offset - 3 * (step_x + 1) - 1
             step = jnp.where(component == 0, step_x, jnp.where(component == 1, step_y, 0))
             start = (place + 3) % 4 * n_border
-            columns = turned[place - first][start : start + n_border]
-            columns = columns + step.astype(jnp.float32) * column_edge
+            rows = in_buf[0, place, :8, :] + step.astype(jnp.float32) * column_edge
+            columns = turned(rows)[start : start + n_border]
             sums = build(groups + place, slots_of(groups + rank), columns, sums)
         return sums
 

time: 17.8 us -> 17.8 us (level)
  no operation moved by 1% of the time
where the time goes in v6:
time: 17.8 us; the launch traced here: 17.6 us
  Pallas kernels  17 us (96%)
  between operations  0.64 us (4%)
    pallas_call x1, Pallas kernels, shards(): pl.pallas_call(functools.partial(kernel, lax.axis_size('gx'), lax.axis_si...  16.3 us
    pallas_call x1, Pallas kernels, shards(): pl.pallas_call(deliver, out_shape=(flat,) * 4, in_specs=[vmem] * 4, out_s...  0.65 us

profile of v6, /device:TPU:1, one launch (start us, length us, event | category | flops | bytes accessed | tf_op | source)
XLA Modules:
  0.0 17.6 jit_solution(6610386837989938448)
XLA Ops:
  0.6 16.3 %chebyshev.1 = (f32[24,128]{1,0:T(8,128)S(1)}, f32[24,128]{1,0:T(8,128)S(1)}, f32[24,128]{1,0:T(8,128)S(1)}, f32[24,128]{1,0:T(8,128)S(1)}) custom-call(f32[3,1,128]{2,1,0:T(1,128)} %bitcast.25, f32[1,128]{1,0:T(1,128)} %bitcast.26, s32[1,32]{1,0:T(1,128)} %bitcast.27, s32[64,128]{1,0:T(8,128)} %bitcast.20, f32[24,128]{1,0:T(8,128)} %bitcast.21, ...), custom_call_target="tpu_custom_call" | custom-call | tf_op jit(solution)/shard_map/chebyshev/pallas_call | solution.py:322
  17.0 0.7 %deliver.1 = (f32[24,128]{1,0:T(8,128)}, f32[24,128]{1,0:T(8,128)}, f32[24,128]{1,0:T(8,128)}, f32[24,128]{1,0:T(8,128)}) custom-call(f32[24,128]{1,0:T(8,128)S(1)} %get-tuple-element.12.refs_0_, f32[24,128]{1,0:T(8,128)S(1)} %get-tuple-element.13.refs_1_, f32[24,128]{1,0:T(8,128)S(1)} %get-tuple-element.14.refs_2_, f32[24,128]{1,0:T(8,128)S(1)} %get-tuple-element.15.refs_3_), custom_call_target="tpu_custom_call" | custom-call | tf_op jit(solution)/shard_map/deliver/pallas_call | solution.py:358

commit v7 on v6

--- a/solution.py
+++ b/solution.py
@@ -144,6 +144,11 @@
     state_one = fields(field_buf[0], field_buf[1])
     pack(0, state_one + [geometry])
 
+    pl.semaphore_wait(barrier, 8)
+    first = copies(0)
+    for copy in first:
+        copy.start()
+
     loads[7].wait()
     entries = nbr_ref[...]
     shift = n_atoms.bit_length() - 1
@@ -175,11 +180,6 @@
             row = (4 * g + f) * n_border
             part = words[g * n_border : (g + 1) * n_border]
             times_buf[row : row + n_border] = ((part >> (8 * f)) & 255).astype(jnp.float32)
-
-    pl.semaphore_wait(barrier, 8)
-    first = copies(0)
-    for copy in first:
-        copy.start()
 
     picked = lax.broadcasted_iota(jnp.int32, (24, 4 * n_atoms), 0) % 8
     lane_part = lax.broadcasted_iota(jnp.int32, (24, 4 * n_atoms), 1) // n_atoms

time: 17.8 us -> 17.8 us (level)
  no operation moved by 1% of the time
where the time goes in v7:
time: 17.8 us; the launch traced here: 17.6 us
  Pallas kernels  17 us (96%)
  between operations  0.64 us (4%)
    pallas_call x1, Pallas kernels, shards(): pl.pallas_call(functools.partial(kernel, lax.axis_size('gx'), lax.axis_si...  16.3 us
    pallas_call x1, Pallas kernels, shards(): pl.pallas_call(deliver, out_shape=(flat,) * 4, in_specs=[vmem] * 4, out_s...  0.65 us

profile of v7, /device:TPU:1, one launch (start us, length us, event | category | flops | bytes accessed | tf_op | source)
XLA Modules:
  0.0 17.6 jit_solution(79296697835020863)
XLA Ops:
  0.6 16.3 %chebyshev.1 = (f32[24,128]{1,0:T(8,128)S(1)}, f32[24,128]{1,0:T(8,128)S(1)}, f32[24,128]{1,0:T(8,128)S(1)}, f32[24,128]{1,0:T(8,128)S(1)}) custom-call(f32[3,1,128]{2,1,0:T(1,128)} %bitcast.25, f32[1,128]{1,0:T(1,128)} %bitcast.26, s32[1,32]{1,0:T(1,128)} %bitcast.27, s32[64,128]{1,0:T(8,128)} %bitcast.20, f32[24,128]{1,0:T(8,128)} %bitcast.21, ...), custom_call_target="tpu_custom_call" | custom-call | tf_op jit(solution)/shard_map/chebyshev/pallas_call | solution.py:322
  17.0 0.7 %deliver.1 = (f32[24,128]{1,0:T(8,128)}, f32[24,128]{1,0:T(8,128)}, f32[24,128]{1,0:T(8,128)}, f32[24,128]{1,0:T(8,128)}) custom-call(f32[24,128]{1,0:T(8,128)S(1)} %get-tuple-element.12.refs_0_, f32[24,128]{1,0:T(8,128)S(1)} %get-tuple-element.13.refs_1_, f32[24,128]{1,0:T(8,128)S(1)} %get-tuple-element.14.refs_2_, f32[24,128]{1,0:T(8,128)S(1)} %get-tuple-element.15.refs_3_), custom_call_target="tpu_custom_call" | custom-call | tf_op jit(solution)/shard_map/deliver/pallas_call | solution.py:358
